TPU v7x, 32 devices: a whole 2x2x4 slice. The times are simulated.
32 devices in a mesh: gx: 4 (over y, x), gy: 4 (over z), gz: 2 (over core).
Axes of the slice: x: 2, y: 2, z: 4, core: 2. Of those that a mesh axis runs over, the one named last changes fastest.
Arguments:
- boxes: bfloat16 [4, 4, 2, 16, 16, 256], P('gx', 'gy', 'gz'), may hold values from 0 to 2
- anchors: int32 [4, 4, 2, 16, 3], P('gx', 'gy', 'gz'), may hold values from 0 to 4, as said below
- potential: float32 [160, 160, 80], P('gx', 'gy', 'gz'), may hold values from 0.5 to 2
Outputs:
- relaxed: bfloat16 [4, 4, 2, 16, 16, 256], P('gx', 'gy', 'gz')
Inputs may be any that keep to these rules, and one draw needn't show every extreme that they name: `anchors`: in every region exactly 8 of the 16 functions are border functions, and every coordinate of theirs is 0 or 4; all coordinates of the others lie within 1 to 3.
All inputs are finite; a program needn't handle non-finite values.
Results may differ from a plain program's by a relative error of at most 0.0041.
Values may be sent and summed in bfloat16 or wider, within the bound.
A program may use at most 128 MiB of HBM per device.

v0:
```python
import functools

import jax
import jax.numpy as jnp
import ml_dtypes
import numpy as np
from jax import lax
from jax.experimental import pallas as pl
from jax.experimental.pallas import tpu as pltpu
from jax.sharding import PartitionSpec as P

REGION = 5
SWEEPS = 2
MAGIC = [
    8.433424733352934e-07,
    -1.290557201342061e-05,
    8.76298447621056e-05,
    -0.00030158038132690465,
    0.001747237136729939,
    -0.009420470302010804,
    0.023738214637249424,
    0.0612625895831208,
    0.9940415697834004,
    -0.06048952891969835,
    -0.021030251609303816,
    0.013372634148547948,
    -0.0034412814449349387,
    0.0004944322768868992,
    -5.185986881173433e-05,
    2.7273449291197967e-06,
]
KINETIC = [
    -3.55369228991319,
    2.2191465938911166,
    -0.6156141465570069,
    0.2371780582153806,
    -0.0822663999742123,
    0.0220702918848226,
    -0.004097656893426338,
    0.00045167920287502236,
    -2.3982285245075998e-05,
    2.0904234952920368e-06,
    -3.7230763047369276e-07,
    -1.0585705549674146e-08,
    -5.8138798302825403e-11,
    2.7080049362631943e-13,
    -6.9244749406392e-18,
]
CELL = 1.0 / 4096.0
STEP = 0.1
PENALTY = 3.0
BF = jnp.bfloat16
F32 = jnp.float32
MESH = pl.DeviceIdType.MESH
CYCLE = ((0, 0), (0, 1), (1, 1), (1, 0))
AXES = ("gx", "gy", "gz")

PCOL, PCOLT, RM, RK, RMT, LM, LMT, LK = range(8)


def rounded(table):
    return table.astype(np.float32).astype(ml_dtypes.bfloat16).astype(np.float64)


def best_scale(table):
    tried = 1.0 + np.arange(2048) / 2048.0
    wrong = [np.square(rounded(table * t) / t - table).sum() for t in tried]
    return tried[int(np.argmin(wrong))]


def make_tables():
    magic = np.zeros((16, 16))
    kinetic = np.zeros((16, 16))
    for r in range(16):
        for c in range(16):
            if -8 <= c - r <= 7:
                magic[r, c] = MAGIC[c - r + 8]
            if abs(c - r) <= 14:
                kinetic[r, c] = KINETIC[abs(c - r)]
    new = np.arange(256)
    py, pz, yy, zz = new // 128, new // 64 % 2, new // 8 % 8, new % 8
    old = (8 * py + yy) * 16 + 8 * pz + zz
    pcol = np.zeros((256, 256))
    pcol[old, new] = 1.0
    eye = np.eye(16)
    rm = np.kron(magic, magic).T[old][:, old]
    rk = -0.5 * (np.kron(kinetic, eye) + np.kron(eye, kinetic))[old][:, old]
    lm = np.kron(magic, eye)
    lk = -0.5 * np.kron(kinetic, eye)
    row = slice(7, 8)
    left = best_scale(magic[row])
    right = best_scale(np.kron(magic[row], magic[row]))
    curve = best_scale(np.concatenate([kinetic[row], 2.0 * kinetic[row]]))
    out = [pcol, pcol.T, rm * right, rk * curve, rm.T * right]
    out += [lm * left, lm.T * left, lk * curve]
    stack = np.stack(out).astype(np.float32).astype(ml_dtypes.bfloat16)
    return stack, float((left * right) ** -2), float(1.0 / curve)


def plan():
    first, messages, slot_of = 4, [], [0] * 4
    for dx in (-1, 0, 1):
        for dy in (-1, 0, 1):
            if dx == dy == 0:
                continue
            ex, ey = -dx, -dy
            px, py = (0 if ex < 0 else 1), (0 if ey < 0 else 1)
            count = (1 if ex else 2) * (1 if ey else 2)
            if ex and ey:
                index = CYCLE.index((px, py))
            elif ex:
                index = 2 * px
            else:
                index = 1 if py else 3
            messages.append(((ex, ey, 0), index, first, count))
            slot_of += [len(messages)] * count
            first += count
    return messages, slot_of


def mm(a, b):
    return jnp.dot(a, b, preferred_element_type=F32)


def mm_nt(a, b):
    return lax.dot_general(a, b, (((1,), (1,)), ((), ())), preferred_element_type=F32)


def iota(shape, dim):
    return lax.broadcasted_iota(jnp.int32, shape, dim)


def to_octants(value):
    rows = []
    for px in range(2):
        for block in range(4):
            rows.append(
                jnp.concatenate(
                    [
                        value[px * 128 + x * 16 : px * 128 + x * 16 + 16, block * 64 : block * 64 + 64]
                        for x in range(8)
                    ],
                    axis=1,
                )
            )
    return jnp.concatenate(rows, axis=0)


def from_octants(value):
    rows = []
    for px in range(2):
        for x in range(8):
            rows.append(
                jnp.concatenate(
                    [
                        value[(px * 4 + block) * 16 : (px * 4 + block) * 16 + 16, x * 64 : x * 64 + 64]
                        for block in range(4)
                    ],
                    axis=1,
                )
            )
    return jnp.concatenate(rows, axis=0)


def kernel(
    counts, messages, scale_v, scale_k,
    box_hbm, anchor_ref, pot_hbm, tables_hbm, same_hbm,
    out_ref,
    box_ref, pot_ref, tab, same, ex1, ex2, recv1, recv2,
    turned, halo, halo_x, hx, hy, hz, hxy, hxz, hyz, hxyz,
    load_sem, send_sem, recv_sem, pass_send, pass_recv, halo_send, halo_recv,
):
    me = [lax.axis_index(name) for name in AXES]

    def device(offset):
        return tuple(
            lax.rem(me[i] + (offset[i] + counts[i]), counts[i]) if offset[i] else me[i]
            for i in range(3)
        )

    ups = (1,) if counts[2] == 2 else (-1, 1)
    low = ups[0]
    reach = {m[0] for m in messages} | {(0, 0, up) for up in ups}
    reach |= {(-1, 0, low), (0, -1, low), (-1, -1, low)}
    reach |= {(1, 0, -low), (0, 1, -low), (1, 1, -low)}
    reach = sorted({(x, y, abs(z) if counts[2] == 2 else z) for x, y, z in reach})
    barrier = pltpu.get_barrier_semaphore()
    for offset in reach:
        pl.semaphore_signal(barrier, inc=1, device_id=device(offset), device_id_type=MESH)

    loads = [
        pltpu.make_async_copy(src, dst, load_sem.at[n])
        for n, (src, dst) in enumerate(
            [
                (pot_hbm, pot_ref),
                (box_hbm, box_ref),
                (tables_hbm.at[pl.ds(0, 2)], tab.at[pl.ds(0, 2)]),
                (tables_hbm.at[pl.ds(2, 6)], tab.at[pl.ds(2, 6)]),
                (same_hbm, same),
            ]
        )
    ]
    for load in loads:
        load.start()

    row_f = iota((16, 128), 0)
    lane_f = iota((16, 128), 1) % 16
    coord = []
    for i in range(3):
        along = anchor_ref[0, 0, i].astype(F32)
        square = jnp.where(iota((16, 16), 0) == iota((16, 16), 1), along, 0.0)
        coord.append(jnp.sum(square, axis=1, keepdims=True).astype(jnp.int32))
    touch = functools.reduce(
        jnp.maximum,
        [((c == 0) | (c == REGION - 1)).astype(F32) for c in coord],
    )
    rank = jnp.sum(jnp.where(row_f < lane_f, touch, 0.0), axis=0, keepdims=True)
    touched = jnp.sum(jnp.where(row_f == lane_f, touch, 0.0), axis=0, keepdims=True)
    row_s = iota((80, 128), 0)
    lane_s = iota((80, 128), 1)
    slab = row_s // 16
    octant = jnp.where(slab == 4, 0, jnp.where(slab == 2, 3, jnp.where(slab == 3, 2, slab)))
    octant = octant * 2 + row_s // 8 % 2
    select = jnp.where(
        (octant == lane_s // 16) & ((row_s % 8).astype(F32) == rank) & (touched > 0.5), 1.0, 0.0
    ).astype(BF)
    lanes = iota((16, 128), 1)
    hots = []
    for p in range(8):
        hot, first = None, 0
        for i, bit in enumerate((p // 4, p // 2 % 2, p % 2)):
            span = REGION * counts[i]
            value = coord[i] + (me[i] * REGION + bit)
            value = jnp.where(value >= span, value - span, value) + first
            part = (lanes == value).astype(F32)
            hot = part if hot is None else hot + part
            first += span
        hots.append(hot)
    hot = jnp.concatenate(hots, axis=0).astype(BF)

    loads[0].wait()
    z = iota((40, 384), 0)
    lane = iota((40, 384), 1)
    base = lane - ((z // 8) * 64 + z % 8)
    own = None
    for y in range(8):
        picked = jnp.concatenate(
            [pot_ref[pl.ds(by * 8 + y, 40, stride=40), :] for by in range(5)], axis=0
        ).astype(BF)
        part = mm(picked, (base == 8 * y).astype(F32).astype(BF))
        own = part if own is None else own + part
    for by in range(5):
        halo[by] = jnp.concatenate(
            [own[by * 40 : by * 40 + 40], jnp.zeros((8, 384), F32)], axis=0
        ).astype(BF)

    halo_x[...] = jnp.concatenate(
        [own[by * 40 : by * 40 + 8] for by in range(5)] + [jnp.zeros((8, 384), F32)], axis=0
    ).astype(BF)
    pl.semaphore_wait(barrier, len(reach))
    def remote(src, dst, send, recv, offset):
        return pltpu.make_async_remote_copy(
            src_ref=src, dst_ref=dst, send_sem=send, recv_sem=recv,
            device_id=device(offset), device_id_type=MESH,
        )

    halos = [
        remote(src, dst, halo_send.at[n], halo_recv.at[n], offset)
        for n, (src, dst, offset) in enumerate(
            [
                (halo_x, hx, (-1, 0, 0)),
                (halo.at[pl.ds(0, 1)], hy, (0, -1, 0)),
                (halo.at[:, :, pl.ds(0, 128)], hz, (0, 0, low)),
                (halo_x.at[pl.ds(0, 16)], hxy, (-1, -1, 0)),
                (halo_x.at[:, pl.ds(0, 128)], hxz, (-1, 0, low)),
                (halo.at[pl.ds(0, 1), :, pl.ds(0, 128)], hyz, (0, -1, low)),
                (halo_x.at[pl.ds(0, 16), pl.ds(0, 128)], hxyz, (-1, -1, low)),
            ]
        )
    ]
    for copy in halos:
        copy.start()

    loads[1].wait()
    loads[2].wait()
    permuted = mm(box_ref[...], tab[PCOL])
    halves = []
    for half in range(2):
        turned[half] = permuted[:, half * 128 : half * 128 + 128]
        halves.append(
            jnp.concatenate([turned[half, pl.ds(x, 16, stride=16), :] for x in range(16)], axis=0)
        )
    current_f = jnp.concatenate(halves, axis=1)

    def spread(sweep, source, target):
        for offset, index, first, count in messages:
            remote(
                source.at[pl.ds(index, count)], target.at[0, pl.ds(first, count)],
                send_sem.at[sweep], recv_sem.at[sweep], offset,
            ).start()
        landed = target.at[0, pl.ds(4, 12)]
        copies = [remote(landed, landed, send_sem.at[sweep], recv_sem.at[sweep], (1, 0, 0))]
        own = [
            remote(
                source.at[pl.ds(0, 4)], target.at[2 * n, pl.ds(0, 4)],
                pass_send.at[sweep, 0, n], pass_recv.at[sweep, 0, n], (0, 0, -up if counts[2] > 2 else up),
            )
            for n, up in enumerate(ups)
        ]
        for copy in own:
            copy.start()
        return copies, own

    def pass_on(sweep, target):
        copies = [
            remote(
                target.at[0, pl.ds(4, 12)], target.at[1 + n, pl.ds(4, 12)],
                pass_send.at[sweep, 1, n], pass_recv.at[sweep, 1, n], (0, 0, -up if counts[2] > 2 else up),
            )
            for n, up in enumerate(ups)
        ]
        for copy in copies:
            copy.start()
        return copies

    def export(sweep, octs):
        if sweep == 0:
            listed = mm(select, jnp.concatenate([octs, hot], axis=1))
            ex1[...] = listed.astype(BF).reshape(5, 16, 640)
            return spread(0, ex1, recv1)
        ex2[...] = mm(select, octs).astype(BF).reshape(5, 16, 512)
        return spread(1, ex2, recv2)

    current = current_f.astype(BF)
    octs_f = to_octants(current_f)
    octs = octs_f.astype(BF)
    copies, owns = export(0, octs)

    mask_own = mm_nt(hot, hot) > 2.5
    same_own = (iota((128, 128), 0) % 16 == iota((128, 128), 1) % 16).astype(F32).astype(BF)
    delta = jnp.where(row_f == lane_f, PENALTY, 0.0)
    sent = list(halos)

    def weights(overlap, mask, table, extra):
        width = overlap.shape[1]
        kept = jnp.where(mask, overlap, 0.0).reshape(8, 16, width).sum(axis=0)
        high = kept.astype(BF).astype(F32)
        both = mm(jnp.concatenate([high, kept - high], axis=0).astype(BF), table)
        coupling = (both[:16] + both[16:]) * CELL
        if extra is not None:
            coupling = coupling + extra
        copied = jnp.concatenate([coupling] * 8, axis=0)
        return jnp.where(mask, copied, 0.0).astype(BF)

    masks = []
    potential = None
    for sweep in range(SWEEPS):
        if sweep:
            copies, owns = export(sweep, octs)
            current = from_octants(octs_f).astype(BF)
        target = recv1 if sweep == 0 else recv2

        if sweep == 0:
            loads[3].wait()
        on_grid = mm(tab[LM], mm(current, tab[RM]).astype(BF))
        kinetic = (mm(current, tab[RK]) + mm(tab[LK], current)) * scale_k

        if sweep == 0:
            for copy in halos:
                copy.wait_recv()
            pieces = []
            hx_f, hxz_f = hx[...].astype(F32), hxz[...].astype(F32)
            for by in range(6):
                if by < 5:
                    a, c = halo[by].astype(F32), hz[by].astype(F32)
                    b, d = hx_f[by * 8 : by * 8 + 8], hxz_f[by * 8 : by * 8 + 8]
                else:
                    a, c = hy[0].astype(F32), hyz[0].astype(F32)
                    b, d = hxy[...].astype(F32)[:8], hxyz[...].astype(F32)[:8]
                body = jnp.concatenate([a[:40], b], axis=0)
                side = jnp.concatenate([c[:40], d], axis=0)
                pieces.append(
                    jnp.concatenate(
                        [body[:, :256], jnp.concatenate([body[:, 256:320], side[:, :64]], axis=1)], axis=1
                    )
                )
            pieces.append(jnp.zeros((96, 384), F32))
            extended = jnp.concatenate(pieces, axis=0).astype(BF)
            column = iota((16, 384), 1)
            blocks = []
            depth = jnp.concatenate([coord[2]] * 16, axis=0)
            for py in range(2):
                start = (coord[1] + py) * 48 + coord[0] * 8
                rows = jnp.concatenate(
                    [(column == start + x).astype(F32) for x in range(16)], axis=0
                ).astype(BF)
                taken = mm(rows, extended)
                block = taken[:, :128]
                for bz in range(1, 5):
                    block = jnp.where(depth == bz, taken[:, bz * 64 : bz * 64 + 128], block)
                blocks.append(block * scale_v)
                if py == 0:
                    for copy in copies:
                        copy.wait_recv()
                    passed = pass_on(sweep, target)
            potential = jnp.concatenate(blocks, axis=1)

        weighted = (potential * on_grid).astype(BF)
        applied = mm(tab[LMT], mm(weighted, tab[RMT]).astype(BF)) + kinetic

        if sweep == 0:
            for copy in owns + passed:
                copy.wait_recv()
            loads[4].wait()
        applied = to_octants(applied)
        mixed = (applied - PENALTY * octs_f).astype(BF)
        w_own = weights(mm_nt(mixed, octs), mask_own, same_own, delta)
        correction = mm(w_own, octs)
        if sweep:
            for copy in sent:
                copy.wait_send()
            for copy in copies:
                copy.wait_recv()
            passed = pass_on(sweep, target)
            for copy in owns:
                copy.wait_recv()
        for group in range(1 + len(ups)):
            if group == 1 and sweep:
                for copy in copies + owns + passed:
                    copy.wait_send()
                for copy in passed:
                    copy.wait_recv()
            skip = 4 if group == 1 else 0
            received = target[group, skip:].reshape(256 - skip * 16, target.shape[3])
            if sweep == 0:
                masks.append(mm_nt(hot, received[:, 512:]) > 2.5)
            received = received[:, :512]
            w_near = weights(mm_nt(mixed, received), masks[group], same[skip * 16 :, skip * 16 :], None)
            correction = correction + mm(w_near, received)
        if sweep == 0:
            sent += copies + owns + passed
        octs = (octs_f - STEP * (applied - correction)).astype(BF)
        octs_f = octs.astype(F32)

    back = mm(from_octants(octs_f).astype(BF), tab[PCOLT])
    for half in range(2):
        for x in range(16):
            turned[half, pl.ds(x, 16, stride=16), :] = back[
                x * 16 : x * 16 + 16, half * 128 : half * 128 + 128
            ]
    out_ref[...] = jnp.concatenate([turned[0], turned[1]], axis=1).astype(BF)


def solution(mesh):
    counts = tuple(mesh.shape[name] for name in AXES)
    messages, slot_of = plan()
    slot = np.repeat(np.array(slot_of), 16)
    item = np.arange(256) % 8
    same = (slot[:, None] == slot[None, :]) & (item[:, None] == item[None, :])
    same = same.astype(np.float32).astype(ml_dtypes.bfloat16)
    tables, scale_v, scale_k = make_tables()
    layers = 2 if counts[2] == 2 else 3
    vmem = pl.BlockSpec(memory_space=pltpu.VMEM)
    anyspace = pl.BlockSpec(memory_space=pl.ANY)

    def local(boxes, anchors, potential):
        shape = boxes.shape
        out = pl.pallas_call(
            functools.partial(kernel, counts, messages, scale_v, scale_k),
            out_shape=jax.ShapeDtypeStruct((256, 256), BF),
            in_specs=[anyspace, vmem, anyspace, anyspace, anyspace],
            out_specs=vmem,
            scratch_shapes=[
                pltpu.VMEM((256, 256), BF),
                pltpu.VMEM((1600, 40), F32),
                pltpu.VMEM(tables.shape, BF),
                pltpu.VMEM(same.shape, BF),
                pltpu.VMEM((5, 16, 640), BF),
                pltpu.VMEM((5, 16, 512), BF),
                pltpu.VMEM((layers, 16, 16, 640), BF),
                pltpu.VMEM((layers, 16, 16, 512), BF),
                pltpu.VMEM((2, 256, 128), F32),
                pltpu.VMEM((5, 48, 384), BF),
                pltpu.VMEM((48, 384), BF),
                pltpu.VMEM((48, 384), BF),
                pltpu.VMEM((1, 48, 384), BF),
                pltpu.VMEM((5, 48, 128), BF),
                pltpu.VMEM((16, 384), BF),
                pltpu.VMEM((48, 128), BF),
                pltpu.VMEM((1, 48, 128), BF),
                pltpu.VMEM((16, 128), BF),
                pltpu.SemaphoreType.DMA((5,)),
                pltpu.SemaphoreType.DMA((SWEEPS,)),
                pltpu.SemaphoreType.DMA((SWEEPS,)),
                pltpu.SemaphoreType.DMA((SWEEPS, 2, 2)),
                pltpu.SemaphoreType.DMA((SWEEPS, 2, 2)),
                pltpu.SemaphoreType.DMA((7,)),
                pltpu.SemaphoreType.DMA((7,)),
            ],
            compiler_params=pltpu.CompilerParams(
                collective_id=0, has_side_effects=True, vmem_limit_bytes=55040 * 1024
            ),
        )(
            boxes.reshape(256, 256),
            jnp.transpose(anchors, (0, 1, 4, 2, 3)),
            potential.reshape(1600, 40),
            jnp.asarray(tables),
            jnp.asarray(same),
        )
        return out.reshape(shape)

    placed = (
        P("gx", "gy", "gz", None, None, None),
        P("gx", "gy", "gz", None, None),
        P("gx", "gy", "gz"),
    )
    return jax.shard_map(
        local,
        mesh=mesh,
        in_specs=placed,
        out_specs=P("gx", "gy", "gz", None, None, None),
        check_vma=False,
    )
```

profile of v0, /device:TPU:0, one launch (start us, length us, event | category | flops | bytes accessed | tf_op | source)
XLA Modules:
  0.0 27.0 jit_solution(7922665584794674675)
XLA Ops:
  0.0 0.0 copy-start
  0.0 0.7 %copy-done = s32[1,1,1,16,3]{3,2,4,1,0:T(1,128)S(1)} copy-done((s32[1,1,1,16,3]{3,2,4,1,0:T(1,128)S(1)}, s32[1,1,1,16,3]{3,2,4,1,0:T(1,128)}, u32[]{:S(2)}) %copy-start) | copy-done | bytes 216
  0.7 25.7 %shard_map.55 = bf16[256,256]{1,0:T(8,128)(2,1)S(1)} custom-call(bf16[256,256]{1,0:T(8,128)(2,1)} %bitcast.7, s32[1,1,3,1,16]{4,3,2,1,0:T(1,128)S(1)} %bitcast.5, f32[1600,40]{1,0:T(8,128)} %bitcast.6, bf16[8,256,256]{2,1,0:T(8,128)(2,1)} %constant.4.clone.tables_hbm, bf16[256,256]{1,0:T(8,128)(2,1)} %constant.5.clone.same_hbm), custom_call_target="tpu_custom_call" | custom-call | tf_op jit(solution)/shard_map/pallas_call | solution.py:468
  26.4 0.7 %copy.7 = bf16[1,1,1,16,16,256]{5,4,3,2,1,0:T(8,128)(2,1)} copy(bf16[1,1,1,16,16,256]{5,4,3,2,1,0:T(8,128)(2,1)S(1)} %bitcast.4) | data formatting | bytes 262144
Async XLA Ops:
  0.0 0.7 %copy-start = (s32[1,1,1,16,3]{3,2,4,1,0:T(1,128)S(1)}, s32[1,1,1,16,3]{3,2,4,1,0:T(1,128)}, u32[]{:S(2)}) copy-start(s32[1,1,1,16,3]{3,2,4,1,0:T(1,128)} %param.6) | copy-start | bytes 580
where the time goes:
time: 27.2 us; the launch traced here: 27 us
  Pallas kernels  25.7 us (94%)
  local copies, waits for them, and re-layouts  1.34 us (5%)
    pallas_call x1, Pallas kernels, local(): pl.pallas_call(functools.partial(kernel, counts, messages, scale_v, scale...  25.7 us
    unnamed x3, local copies, waits for them, and re-layouts  1.34 us

commit v1 on v0

--- a/solution.py
+++ b/solution.py
@@ -115,6 +115,7 @@
             messages.append(((ex, ey, 0), index, first, count))
             slot_of += [len(messages)] * count
             first += count
+    messages.sort(key=lambda m: (m[0][0] * m[0][1] == 0, m[0][1] == 0))
     return messages, slot_of
 
 
@@ -399,17 +400,17 @@
                 for bz in range(1, 5):
                     block = jnp.where(depth == bz, taken[:, bz * 64 : bz * 64 + 128], block)
                 blocks.append(block * scale_v)
-                if py == 0:
-                    for copy in copies:
-                        copy.wait_recv()
-                    passed = pass_on(sweep, target)
             potential = jnp.concatenate(blocks, axis=1)
 
+        if sweep == 0:
+            for copy in copies:
+                copy.wait_recv()
+            passed = pass_on(sweep, target)
         weighted = (potential * on_grid).astype(BF)
         applied = mm(tab[LMT], mm(weighted, tab[RMT]).astype(BF)) + kinetic
 
         if sweep == 0:
-            for copy in owns + passed:
+            for copy in owns:
                 copy.wait_recv()
             loads[4].wait()
         applied = to_octants(applied)
@@ -425,9 +426,10 @@
             for copy in owns:
                 copy.wait_recv()
         for group in range(1 + len(ups)):
-            if group == 1 and sweep:
-                for copy in copies + owns + passed:
-                    copy.wait_send()
+            if group == 1:
+                if sweep:
+                    for copy in copies + owns + passed:
+                        copy.wait_send()
                 for copy in passed:
                     copy.wait_recv()
             skip = 4 if group == 1 else 0

time: 27.2 us -> 25.9 us (0.952)
  Pallas kernels: 25.7 us -> 24.4 us
    pallas_call x1, Pallas kernels: 25.7 us -> 24.4 us  [local(): pl.pallas_call(functools.partial(kernel, counts, messages, scale_v, scale...]
where the time goes in v1:
time: 25.9 us; the launch traced here: 25.8 us
  Pallas kernels  24.4 us (94%)
  local copies, waits for them, and re-layouts  1.34 us (5%)
    pallas_call x1, Pallas kernels, local(): pl.pallas_call(functools.partial(kernel, counts, messages, scale_v, scale...  24.4 us
    unnamed x3, local copies, waits for them, and re-layouts  1.34 us

profile of v1, /device:TPU:0, one launch (start us, length us, event | category | flops | bytes accessed | tf_op | source)
XLA Modules:
  0.0 25.8 jit_solution(14938549734972447652)
XLA Ops:
  0.0 0.0 copy-start
  0.0 0.7 %copy-done = s32[1,1,1,16,3]{3,2,4,1,0:T(1,128)S(1)} copy-done((s32[1,1,1,16,3]{3,2,4,1,0:T(1,128)S(1)}, s32[1,1,1,16,3]{3,2,4,1,0:T(1,128)}, u32[]{:S(2)}) %copy-start) | copy-done | bytes 216
  0.7 24.4 %shard_map.55 = bf16[256,256]{1,0:T(8,128)(2,1)S(1)} custom-call(bf16[256,256]{1,0:T(8,128)(2,1)} %bitcast.7, s32[1,1,3,1,16]{4,3,2,1,0:T(1,128)S(1)} %bitcast.5, f32[1600,40]{1,0:T(8,128)} %bitcast.6, bf16[8,256,256]{2,1,0:T(8,128)(2,1)} %constant.4.clone.tables_hbm, bf16[256,256]{1,0:T(8,128)(2,1)} %constant.5.clone.same_hbm), custom_call_target="tpu_custom_call" | custom-call | tf_op jit(solution)/shard_map/pallas_call | solution.py:470
  25.1 0.7 %copy.7 = bf16[1,1,1,16,16,256]{5,4,3,2,1,0:T(8,128)(2,1)} copy(bf16[1,1,1,16,16,256]{5,4,3,2,1,0:T(8,128)(2,1)S(1)} %bitcast.4) | data formatting | bytes 262144
Async XLA Ops:
  0.0 0.7 %copy-start = (s32[1,1,1,16,3]{3,2,4,1,0:T(1,128)S(1)}, s32[1,1,1,16,3]{3,2,4,1,0:T(1,128)}, u32[]{:S(2)}) copy-start(s32[1,1,1,16,3]{3,2,4,1,0:T(1,128)} %param.6) | copy-start | bytes 580
